TPU v7x, 128 devices: a whole 4x4x4 slice. The times are simulated.
128 devices in a mesh: blk: 16 (over y_hi, x, core), grp: 8 (over y_lo, z).
Axes of the slice: x: 4, y: 4 (y_hi: 2, y_lo: 2; y = y_hi * 2 + y_lo), z: 4, core: 2. Of those that a mesh axis runs over, the one named last changes fastest.
Arguments:
- particles: bfloat16 [12288, 4096], P(('blk', 'grp')), may hold values from -24 to 24
- references: bfloat16 [1536, 4096], P(('blk', 'grp')), may hold values from -6 to 6
- candidates: int32 [12288, 4], P(('blk', 'grp')), may hold values from 0 to 191, as said below
- shifts: int32 [9, 2], replicated, may hold values from -4 to 4, as said below
- class_order: int32 [192], replicated, may hold values from 0 to 191, each once
Outputs:
- new_refs: float32 [192, 4096], P('blk', 'grp')
Inputs may be any that keep to these rules, and one draw needn't show every extreme that they name: Each particle's 4 candidates are different classes. `shifts`: the first translation is zero; some translation is (4, -4).
All inputs are finite; a program needn't handle non-finite values.
Results may differ from a plain program's by a relative error of at most 0.0076.
Values may be sent and summed in bfloat16 or wider, within the bound.
A program may use at most 128 MiB of HBM per device.

v0:
```python
import math

import jax
import jax.numpy as jnp
from jax import lax
from jax.experimental import pallas as pl
from jax.experimental.pallas import tpu as pltpu
from jax.sharding import PartitionSpec as P

BOX = 128
ROT = 8
SCALE = 0.05
HALF = 512
PART = 96
TRANS = 9
ROWS = 896
CLS = 192
REFS = 1536
ORDER = (2, 1, 3, 0)
NT = (((1,), (1,)), ((), ()))
F32 = jnp.float32
BF16 = jnp.bfloat16


def pos_of(offset):
    return ORDER.index(offset % 4)


def kernel(
    parts, refs_in, cand_in, shifts, order_in, out,
    refs_own, parts_own, stage, stage32, refs, refs32, squares, hn, pb, table, sh, cand, cb, cs, order_row, order,
    gather_a, gather_b, e_out, e_in, wb, wt, totals, sums, pair_out, pair_in, msg, fin,
    in_sem, st_send, st_recv, pt_send, pt_recv, cd_send, cd_recv,
    ag_send, ag_recv, sb_send, sb_recv, rs_send, rs_recv, ww_send, ww_recv, pr_send, pr_recv, fn_send, fn_recv,
):
    b = lax.axis_index("blk")
    g = lax.axis_index("grp")
    c = b % 2
    x = (b // 2) % 4
    y = (b // 8) * 2 + g // 4
    z = g % 4

    def dev(x_, y_, c_, z_):
        return (((y_ // 2) * 4 + x_) * 2 + c_, (y_ % 2) * 4 + z_)

    def remote(src, dst, ssem, rsem, device):
        return pltpu.make_async_remote_copy(
            src_ref=src, dst_ref=dst, send_sem=ssem, recv_sem=rsem,
            device_id=device, device_id_type=pl.DeviceIdType.MESH)

    def zdev(delta):
        return dev(x, y, c, (z + delta) % 4)

    def shift_tables():
        index = lax.broadcasted_iota(jnp.int32, (16, HALF), 1) + z * HALF
        row = lax.broadcasted_iota(jnp.int32, (16, HALF), 0)
        turns = jnp.zeros((16, HALF), jnp.int32)
        for t in range(TRANS):
            line = shifts[0, t] * (index % (BOX // 2)) + shifts[1, t] * (index // (BOX // 2))
            turns = jnp.where(row == t, line, turns)
        angle = (turns & (BOX - 1)).astype(F32) * (2.0 * math.pi / BOX)
        table[0] = jnp.cos(angle)
        table[1] = jnp.sin(angle)

    def shift_block(p):
        base = p * ROWS
        sh[base + TRANS * PART:base + ROWS, :] = jnp.zeros((ROWS - TRANS * PART, 2 * HALF), BF16)

        def group(q, _):
            rows = pl.ds(pl.multiple_of(q * 16, 16), 16)
            if p == 3:
                re = parts_own[rows, pl.ds(pl.multiple_of(z * HALF, HALF), HALF)].astype(F32)
                im = parts_own[rows, pl.ds(pl.multiple_of(2048 + z * HALF, HALF), HALF)].astype(F32)
            else:
                re = pb[p, 0, rows, :].astype(F32)
                im = pb[p, 1, rows, :].astype(F32)
            for t in range(TRANS):
                co = table[0, t:t + 1, :]
                si = table[1, t:t + 1, :]
                row = base + q * 128 + t * 16 if t < 8 else base + 768 + q * 16
                dst = pl.ds(pl.multiple_of(row, 16), 16)
                sh[dst, 0:HALF] = (re * co - im * si).astype(BF16)
                sh[dst, HALF:2 * HALF] = (re * si + im * co).astype(BF16)
            return 0

        lax.fori_loop(0, 6, group, 0)

    barrier = pltpu.get_barrier_semaphore()

    def greet(device):
        pl.semaphore_signal(barrier, inc=1, device_id=device, device_id_type=pl.DeviceIdType.MESH)

    for k in (1, 2, 3):
        greet(dev((x + k) % 4, y, c, z))
        greet(dev(x, (y + k) % 4, c, z))
    for dz in (1, 2, 3):
        for dc in (0, 1):
            greet(dev(x, y, (c + dc) % 2, (z + dz) % 4))
    greet(dev(x, y, 1 - c, z))
    load_cand = pltpu.make_async_copy(cand_in, cand, in_sem.at[0])
    load_cand.start()
    load_order = pltpu.make_async_copy(order_in, order_row, in_sem.at[1])
    load_order.start()

    load_refs = pltpu.make_async_copy(refs_in, refs_own, in_sem.at[6])
    load_refs.start()
    load_parts = pltpu.make_async_copy(parts, parts_own, in_sem.at[7])
    load_parts.start()

    load_refs.wait()
    pl.semaphore_wait(barrier, 13)

    def stage_copy(dc, dz):
        k = dc * 4 + dz
        c_ = (c + dc) % 2
        z_ = (z + dz) % 4
        cols = pl.ds(pl.multiple_of(c_ * 2048 + z_ * 512, 512), 512)
        return remote(refs_own.at[:, cols], stage.at[c * 4 + z], st_send.at[k], st_recv.at[k],
                      dev(x, y, c_, z_))

    stage_offsets = [(dc, dz) for dz in (2, 1, 3, 0) for dc in (0, 1) if dc or dz]
    for dc, dz in stage_offsets:
        stage_copy(dc, dz).start()
    own_cols = pl.ds(pl.multiple_of(c * 2048 + z * 512, 512), 512)
    stage[c * 4 + z] = refs_own[:, own_cols]

    def part_copy(dz, h):
        z_ = (z + dz) % 4
        cols = pl.ds(pl.multiple_of(h * 2048 + z_ * 512, 512), 512)
        p = pos_of(-dz)
        return remote(parts_own.at[:, cols], pb.at[p, h], pt_send.at[p * 2 + h], pt_recv.at[p * 2 + h], zdev(dz))

    def cand_copy(dz):
        p = pos_of(-dz)
        return remote(cb.at[3], cb.at[p], cd_send.at[p], cd_recv.at[p], zdev(dz))

    for dc, dz in stage_offsets:
        stage_copy(dc, dz).wait_recv()
    for i in range(8):
        stage32[i * 12:(i + 1) * 12, :] = stage[i].astype(F32)

    def block_rows(x_, y_):
        return pl.ds(pl.multiple_of((x_ * 4 + y_) * 96, 96), 96)

    refs[c, block_rows(x, y), :] = stage32[...].astype(BF16)

    def at(a, b_, core=None):
        core = c if core is None else core
        dx = a * (1 - core) + b_ * core
        dy = b_ * (1 - core) + a * core
        return (x + dx) % 4, (y + dy) % 4

    def ref_block(a, b_):
        x_, y_ = at(a, b_)
        return refs.at[c, block_rows(x_, y_), :]

    def first_send(k):
        x_, y_ = at(k, 0)
        block = ref_block(0, 0)
        return remote(block, block, ag_send.at[k], ag_recv.at[((-k) % 4) * 4], dev(x_, y_, c, z))

    def second_send(a, k):
        x_, y_ = at(0, k)
        block = ref_block(a, 0)
        return remote(block, block, ag_send.at[3 + a * 3 + k], ag_recv.at[a * 4 + (-k) % 4], dev(x_, y_, c, z))

    def recv_block(a, b_):
        block = ref_block(a, b_)
        remote(block, block, ag_send.at[0], ag_recv.at[a * 4 + b_], dev(x, y, 1 - c, z)).wait_recv()

    def sib_copy(a, b_):
        block = ref_block(a, b_)
        return remote(block, block, sb_send.at[a * 4 + b_], sb_recv.at[a * 4 + b_], dev(x, y, 1 - c, z))

    for k in (2, 1, 3):
        first_send(k).start()
    sib_copy(0, 0).start()
    load_parts.wait()
    for dz in (1, 3, 2):
        for h in (0, 1):
            part_copy(dz, h).start()
    load_cand.wait()
    own = cand[...]
    lanes = [jnp.concatenate([own[:, q * 16:q * 16 + 16]] * 8, axis=1) for q in range(6)]
    lanes.append(jnp.concatenate([own, jnp.full((4, 32), -1, jnp.int32)], axis=1))
    cb[3, 0:4, :] = jnp.concatenate(lanes, axis=1)
    for dz in (1, 3, 2):
        cand_copy(dz).start()

    shift_tables()
    shift_block(3)
    for k in (2, 1, 3):
        first_send(k).wait_send()
    for k in (2, 1, 3):
        second_send(0, k).start()

    def widen(h, x_, y_, finish=False):
        for core in (0, 1):
            src = pl.ds(pl.multiple_of((x_ * 4 + y_) * 96 + core * 48, 48), 48)
            dst = pl.ds(((((y_ // 2) * 4 + x_) * 2 + core) * 2 + y_ % 2) * 6, 6)
            acc = jnp.zeros((48, 128), F32)
            for j in range(HALF // 128):
                v = refs[h, src, j * 128:(j + 1) * 128].astype(F32)
                refs32[h, dst, :, j * 128:(j + 1) * 128] = v.reshape(6, ROT, 128)
                acc = acc + v * v
            acc = acc.reshape(6, ROT, 128)
            if finish:
                total = 0.5 * jnp.sum(squares[dst] + acc, axis=2, keepdims=True)
                hn[dst] = jnp.broadcast_to(total, (6, ROT, 128))
            else:
                squares[dst] = acc

    for a in (1, 3, 2):
        recv_block(a, 0)
        for k in (2, 1, 3):
            second_send(a, k).start()
        sib_copy(a, 0).start()
    for a in range(4):
        widen(c, *at(a, 0))
    for b_ in (1, 3, 2):
        recv_block(0, b_)
        sib_copy(0, b_).start()
        widen(c, *at(0, b_))

    load_order.wait()
    row_id = lax.broadcasted_iota(jnp.int32, (16, 128), 0)
    lane_id = lax.broadcasted_iota(jnp.int32, (16, 128), 1)
    first = jnp.broadcast_to(order_row[:, 0:128], (16, 128)).astype(F32)
    rest_order = jnp.concatenate([order_row[:, 128:CLS], jnp.full((1, 256 - CLS), -1, jnp.int32)], axis=1)
    second = jnp.broadcast_to(rest_order, (16, 128)).astype(F32)
    for i in range(16):
        start = ((i % 8) * 2 + i // 8) * 12
        here = jnp.where(lane_id == start + row_id, first, 0.0)
        here = here + jnp.where(lane_id + 128 == start + row_id, second, 0.0)
        column = jnp.broadcast_to(jnp.sum(here, axis=1, keepdims=True), (16, 128))
        order[i * 16:i * 16 + 16, :] = jnp.where(row_id < 12, column, -2.0)

    for dz in (1, 3, 2):
        for h in (0, 1):
            part_copy(dz, h).wait_recv()
        cand_copy(dz).wait_recv()
        shift_block(pos_of(-dz))
        for b_ in (1, 3, 2):
            recv_block(dz, b_)
            sib_copy(dz, b_).start()
            widen(c, *at(dz, b_))
    for p in range(4):
        pltpu.make_async_copy(cb.at[p, :, pl.ds(768, 128)], cs.at[p], in_sem.at[2 + p]).start()
    arrivals = [(a, 0) for a in (0, 1, 3, 2)] + [(0, b_) for b_ in (1, 3, 2)]
    arrivals += [(a, b_) for a in (1, 3, 2) for b_ in (1, 3, 2)]
    for a, b_ in arrivals:
        sib_copy(a, b_).wait_recv()
        widen(1 - c, *at(a, b_, 1 - c), True)
    for p in range(4):
        pltpu.make_async_copy(cb.at[p, :, pl.ds(768, 128)], cs.at[p], in_sem.at[2 + p]).wait()

    def rs_copy(p):
        return remote(e_out.at[p], e_in.at[p], rs_send.at[p], rs_recv.at[p], zdev(ORDER[p]))

    def gather(dst, p, q):
        for i in range(16):
            for s in (0, 2):
                first = cs[p, s, q * 16 + i]
                second = cs[p, s + 1, q * 16 + i]
                row = i * 32 + s * 8
                for h in (0, 1):
                    both = jnp.concatenate([refs32[h, first], refs32[h, second]], axis=0)
                    dst[row:row + 16, h * HALF:(h + 1) * HALF] = both.astype(BF16)

    tile_lane = lax.broadcasted_iota(jnp.int32, (8, 128), 1)

    def score(src, p, q, last):
        base = p * ROWS
        moved = jnp.concatenate(
            [sh[pl.ds(pl.multiple_of(base + q * 128, 128), 128), :],
             sh[pl.ds(pl.multiple_of(base + 768, 128), 128), :]], axis=0)
        raw = lax.dot_general(src[...], moved, NT, preferred_element_type=F32)
        main = [jnp.zeros((8, 128), F32) for _ in range(4)]
        for i in range(16):
            in_main = (tile_lane & 15) == i
            in_last = tile_lane == q * 16 + i
            for s in range(4):
                row = i * 32 + s * 8
                norm = hn[cs[p, s, q * 16 + i]]
                main[s] = jnp.where(in_main, raw[row:row + 8, 0:128] - norm, main[s])
                last[s] = jnp.where(in_last, raw[row:row + 8, 128:256] - norm, last[s])
        for s in range(4):
            e_out[p, s * 8:s * 8 + 8, q * 128:q * 128 + 128] = main[s]
        return last

    gather(gather_a, 0, 0)

    def scores(p, _):
        last = [jnp.zeros((8, 128), F32) for _ in range(4)]
        for q in range(6):
            here, ahead = (gather_a, gather_b) if q % 2 == 0 else (gather_b, gather_a)
            if q < 5:
                gather(ahead, p, q + 1)
            else:
                gather(ahead, jnp.minimum(p + 1, 3), 0)
            last = score(here, p, q, last)
        for s in range(4):
            e_out[p, s * 8:s * 8 + 8, 768:896] = last[s]
        for k in range(3):
            @pl.when(p == k)
            def _():
                rs_copy(k).start()
        return 0

    lax.fori_loop(0, 4, scores, 0)

    for p in range(3):
        rs_copy(p).wait_recv()
    low = -1e30
    lane1 = lax.broadcasted_iota(jnp.int32, (8, 128), 1)
    row1 = lax.broadcasted_iota(jnp.int32, (8, 128), 0)

    def fold(rows, op, fill):
        wide = jnp.concatenate(rows[0:6] + [rows[5], rows[5]], axis=0)
        for step in (64, 32, 16):
            wide = op(wide, pltpu.roll(wide, step, 1))
        shifted = [rows[6]] + [pltpu.roll(rows[6], 128 - 16 * q, 1) for q in range(1, 6)]
        rest = jnp.concatenate(shifted + [shifted[5], shifted[5]], axis=0)
        rest = jnp.where(lane1 < 16, rest, fill)
        for step in (16, 32, 64):
            rest = op(rest, pltpu.roll(rest, step, 1))
        wide = op(wide, rest)
        final = jnp.sum(jnp.where((lane1 >> 4) == row1, wide, 0.0), axis=0, keepdims=True)
        return [wide[q:q + 1, :] for q in range(6)] + [final]

    logits = []
    for l in range(7):
        cols = slice(l * 128, l * 128 + 128)
        logits.append(SCALE * (e_out[3, :, cols] + e_in[0, :, cols] + e_in[1, :, cols] + e_in[2, :, cols]))
    top = fold([jnp.max(v, axis=0, keepdims=True) for v in logits], jnp.maximum, low)
    expo = [jnp.exp(v - t) for v, t in zip(logits, top)]
    total = fold([jnp.sum(v, axis=0, keepdims=True) for v in expo], jnp.add, 0.0)
    for l in range(7):
        rows = [jnp.sum(expo[l][s * 8:s * 8 + 8, :], axis=0, keepdims=True) for s in range(4)]
        weight = jnp.concatenate(rows + rows, axis=0) / total[l]
        if l == 6:
            weight = jnp.where(lane1 < PART, weight, 0.0)
        wb[3, :, l * 128:l * 128 + 128] = weight

    def weight_copy(dz):
        p = pos_of(-dz)
        return remote(wb.at[3], wb.at[p], ww_send.at[p], ww_recv.at[p], zdev(dz))

    for dz in (2, 1, 3):
        weight_copy(dz).start()
    def spread(p, first):
        for l in range(7):
            cols = slice(l * 128, l * 128 + 128)
            cls = [jnp.broadcast_to(cb[p, s:s + 1, cols], (8, 128)).astype(F32) for s in range(4)]
            val = [jnp.broadcast_to(wb[p, s:s + 1, cols], (8, 128)) for s in range(4)]
            for r in range(0, 256, 16):
                both = []
                for half in (r, r + 8):
                    rows = order[half:half + 8, :]
                    acc = jnp.zeros((8, 128), F32)
                    for s in range(4):
                        acc = jnp.where(cls[s] == rows, val[s], acc)
                    if first and l == 0:
                        totals[half:half + 8, :] = acc
                    else:
                        totals[half:half + 8, :] += acc
                    both.append(acc)
                wt[r:r + 16, p * ROWS + l * 128:p * ROWS + l * 128 + 128] = jnp.concatenate(both, axis=0).astype(BF16)

    spread(3, True)
    for dz in (1, 3, 2):
        weight_copy(dz).wait_recv()
        spread(pos_of(-dz), False)

    extra = []
    for i in range(16):
        column = jnp.broadcast_to(jnp.sum(totals[i * 16:i * 16 + 16, :], axis=1, keepdims=True), (16, 128))
        line = jnp.sum(jnp.where(row_id == lane_id, column, 0.0), axis=0, keepdims=True)
        high = line.astype(BF16).astype(F32)
        low = line - high
        extra.append(jnp.where(row_id == 12, high, jnp.where(row_id == 13, low, 0.0)))
    extra = jnp.concatenate(extra, axis=0)

    wide_row = lax.broadcasted_iota(jnp.int32, (256, 128), 0) % 16
    mine = pl.ds(pl.multiple_of(c * 128, 128), 128)
    theirs = pl.ds(pl.multiple_of((1 - c) * 128, 128), 128)

    def pair_copy(h):
        return remote(pair_out.at[h], pair_in.at[h], pr_send.at[h], pr_recv.at[h], dev(x, y, 1 - c, z))

    for h in (0, 1):
        for j in range(2):
            col = h * HALF + j * 256
            part_sum = jnp.dot(wt[...], sh[:, col:col + 256], preferred_element_type=F32)
            if j == 0:
                sums[h, :, 0:128] = jnp.where(wide_row < 12, part_sum[:, 0:128], extra)
                sums[h, :, 128:256] = part_sum[:, 128:256]
            else:
                sums[h, :, 256:512] = part_sum
        pair_out[h] = sums[h, theirs, :].astype(BF16)
        pair_copy(h).start()

    me16 = x * 4 + y

    def final_copy(i):
        x_, y_ = i // 4, i % 4
        rows = pl.ds(pl.multiple_of(((y_ // 2) * 4 + x_) * 16, 16), 16)
        return remote(msg.at[y_ % 2, rows, :], fin.at[me16], fn_send.at[i], fn_recv.at[me16], dev(x_, y_, c, z))

    def send_final(h, j):
        i = ((x + 2 + j // 2) % 4) * 4 + ((y // 2 + 1 + j) % 2) * 2 + h

        @pl.when(i != me16)
        def _():
            final_copy(i).start()

        return 0

    for h in (0, 1):
        pair_copy(h).wait_recv()
        both = sums[h, mine, :] + pair_in[h].astype(F32)
        msg[h, :, 128:HALF] = both[:, 128:HALF].astype(BF16)
        first = both[:, 0:128]
        whole = first + pltpu.roll(first, 127, 0)
        high = whole.astype(BF16).astype(F32)
        low = pltpu.roll(whole - high, 1, 0)
        first = jnp.where(wide_row[0:128] == 12, high, jnp.where(wide_row[0:128] == 13, low, first))
        msg[h, :, 0:128] = first.astype(BF16)
        lax.fori_loop(0, 8, lambda j, _: send_final(h, j), 0)

    own_row = pl.ds(pl.multiple_of(((y // 2) * 4 + x) * 16, 16), 16)
    fin[me16] = msg[y % 2, own_row, :]

    def wait_final(i, _):
        @pl.when(i != me16)
        def _():
            remote(fin.at[i], fin.at[i], fn_send.at[i], fn_recv.at[i], dev(x, y, 1 - c, z)).wait_recv()

        return 0

    lax.fori_loop(0, 16, wait_final, 0)

    acc = fin[0].astype(F32)
    for i in range(1, 16):
        acc = acc + fin[i].astype(F32)
    line = acc[12:13, 0:128] + acc[13:14, 0:128]
    den = jnp.sum(jnp.where(row_id == lane_id, jnp.broadcast_to(line, (16, 128)), 0.0), axis=1, keepdims=True) + 1.0
    out[...] = (acc / den)[0:12, :]

    for dc, dz in stage_offsets:
        stage_copy(dc, dz).wait_send()
    for dz in (1, 2, 3):
        for h in (0, 1):
            part_copy(dz, h).wait_send()
        cand_copy(dz).wait_send()
        weight_copy(dz).wait_send()
    for k in (1, 2, 3):
        for a in range(4):
            second_send(a, k).wait_send()
    for a in range(4):
        for b_ in range(4):
            sib_copy(a, b_).wait_send()
    for p in range(3):
        rs_copy(p).wait_send()

    def left_final(i, _):
        @pl.when(i != me16)
        def _():
            final_copy(i).wait_send()

        return 0

    lax.fori_loop(0, 16, left_final, 0)
    for h in (0, 1):
        pair_copy(h).wait_send()


def on_device(particles, references, candidates, shifts, class_order):
    dma = pltpu.SemaphoreType.DMA
    return pl.pallas_call(
        kernel,
        out_shape=jax.ShapeDtypeStruct((12, HALF), F32),
        in_specs=[
            pl.BlockSpec(memory_space=pl.ANY),
            pl.BlockSpec(memory_space=pl.ANY),
            pl.BlockSpec(memory_space=pl.ANY),
            pl.BlockSpec(memory_space=pltpu.SMEM),
            pl.BlockSpec(memory_space=pl.ANY),
        ],
        out_specs=pl.BlockSpec(memory_space=pltpu.VMEM),
        scratch_shapes=[
            pltpu.VMEM((12, 4096), BF16),
            pltpu.VMEM((PART, 4096), BF16),
            pltpu.VMEM((8, 12, HALF), BF16),
            pltpu.VMEM((96, HALF), F32),
            pltpu.VMEM((2, REFS, HALF), BF16),
            pltpu.VMEM((2, CLS, ROT, HALF), F32),
            pltpu.VMEM((CLS, ROT, 128), F32),
            pltpu.VMEM((CLS, ROT, 128), F32),
            pltpu.VMEM((3, 2, PART, HALF), BF16),
            pltpu.VMEM((2, 16, HALF), F32),
            pltpu.VMEM((4 * ROWS, 2 * HALF), BF16),
            pltpu.VMEM((4, PART), jnp.int32),
            pltpu.VMEM((4, 8, ROWS), jnp.int32),
            pltpu.SMEM((4, 8, 128), jnp.int32),
            pltpu.VMEM((1, CLS), jnp.int32),
            pltpu.VMEM((256, 128), F32),
            pltpu.VMEM((512, 2 * HALF), BF16),
            pltpu.VMEM((512, 2 * HALF), BF16),
            pltpu.VMEM((4, 32, ROWS), F32),
            pltpu.VMEM((3, 32, ROWS), F32),
            pltpu.VMEM((4, 8, ROWS), F32),
            pltpu.VMEM((256, 4 * ROWS), BF16),
            pltpu.VMEM((256, 128), F32),
            pltpu.VMEM((2, 256, HALF), F32),
            pltpu.VMEM((2, 128, HALF), BF16),
            pltpu.VMEM((2, 128, HALF), BF16),
            pltpu.VMEM((2, 128, HALF), BF16),
            pltpu.VMEM((16, 16, HALF), BF16),
            dma((8,)),
            dma((8,)), dma((8,)), dma((8,)), dma((8,)), dma((4,)), dma((4,)),
            dma((16,)), dma((16,)), dma((16,)), dma((16,)), dma((3,)), dma((3,)),
            dma((3,)), dma((3,)), dma((2,)), dma((2,)), dma((16,)), dma((16,)),
        ],
        compiler_params=pltpu.CompilerParams(
            collective_id=0, has_side_effects=True, vmem_limit_bytes=int(53.8 * 2**20)),
        name="estep",
    )(particles, references, candidates.T, shifts.T, class_order.reshape(1, CLS))


def solution(mesh):
    return jax.shard_map(
        on_device,
        mesh=mesh,
        in_specs=(
            P(("blk", "grp"), None),
            P(("blk", "grp"), None),
            P(("blk", "grp"), None),
            P(),
            P(),
        ),
        out_specs=P("blk", "grp"),
        check_vma=False,
    )
```

profile of v0, /device:TPU:8, one launch (start us, length us, event | category | flops | bytes accessed | tf_op | source)
XLA Modules:
  0.0 55.5 jit_solution(8097719958071210107)
XLA Ops:
  0.0 0.0 copy-start.2
  0.0 0.0 copy-start
  0.0 0.0 copy-start.1
  0.0 0.7 %copy-done.2 = s32[192]{0:T(256)S(1)} copy-done((s32[192]{0:T(256)S(1)}, s32[192]{0:T(256)}, u32[]{:S(2)}) %copy-start.2) | copy-done | bytes 792
  0.7 0.0 copy-done
  0.7 0.0 copy-done.1
  0.7 54.2 %estep.1 = f32[12,512]{1,0:T(8,128)S(1)} custom-call(bf16[96,4096]{1,0:T(8,128)(2,1)} %parts.1, bf16[12,4096]{1,0:T(8,128)(2,1)} %refs_in.1, s32[4,96]{1,0:T(4,128)S(1)} %bitcast.3, s32[2,9]{1,0:T(2,128)S(1)} %bitcast.4, s32[1,192]{1,0:T(1,128)S(1)} %bitcast.5), custom_call_target="tpu_custom_call" | custom-call | tf_op jit(solution)/shard_map/estep/pallas_call | solution.py:480
  54.9 0.6 %copy.7 = f32[12,512]{1,0:T(8,128)} copy(f32[12,512]{1,0:T(8,128)S(1)} %estep.1) | data formatting | bytes 49152
Async XLA Ops:
  0.0 0.7 %copy-start.2 = (s32[192]{0:T(256)S(1)}, s32[192]{0:T(256)}, u32[]{:S(2)}) copy-start(s32[192]{0:T(256)} %param.9) | copy-start | bytes 2308
  0.0 0.7 %copy-start = (s32[96,4]{0,1:T(4,128)S(1)}, s32[96,4]{0,1:T(4,128)}, u32[]{:S(2)}) copy-start(s32[96,4]{0,1:T(4,128)} %param.7) | copy-start | bytes 4612
  0.0 0.7 %copy-start.1 = (s32[9,2]{0,1:T(2,128)S(1)}, s32[9,2]{0,1:T(2,128)}, u32[]{:S(2)}) copy-start(s32[9,2]{0,1:T(2,128)} %param.8) | copy-start | bytes 220
where the time goes:
time: 55.7 us; the launch traced here: 55.5 us
  Pallas kernels  54.2 us (97%)
  local copies, waits for them, and re-layouts  1.32 us (2%)
    pallas_call x1, Pallas kernels, on_device(): pl.pallas_call(kernel, out_shape=jax.ShapeDtypeStruct((12, HALF), F32), i...  54.2 us
    unnamed x7, local copies, waits for them, and re-layouts  1.32 us

commit v1 on v0

--- a/solution.py
+++ b/solution.py
@@ -235,15 +235,24 @@
         column = jnp.broadcast_to(jnp.sum(here, axis=1, keepdims=True), (16, 128))
         order[i * 16:i * 16 + 16, :] = jnp.where(row_id < 12, column, -2.0)
 
-    for dz in (1, 3, 2):
+    def take_blocks(a):
+        for b_ in (1, 3, 2):
+            recv_block(a, b_)
+            sib_copy(a, b_).start()
+            widen(c, *at(a, b_))
+
+    def take_particles(dz):
         for h in (0, 1):
             part_copy(dz, h).wait_recv()
         cand_copy(dz).wait_recv()
         shift_block(pos_of(-dz))
-        for b_ in (1, 3, 2):
-            recv_block(dz, b_)
-            sib_copy(dz, b_).start()
-            widen(c, *at(dz, b_))
+
+    take_blocks(1)
+    take_particles(1)
+    take_blocks(3)
+    take_particles(3)
+    take_particles(2)
+    take_blocks(2)
     for p in range(4):
         pltpu.make_async_copy(cb.at[p, :, pl.ds(768, 128)], cs.at[p], in_sem.at[2 + p]).start()
     arrivals = [(a, 0) for a in (0, 1, 3, 2)] + [(0, b_) for b_ in (1, 3, 2)]

time: 55.7 us -> 55.7 us (level)
  no operation moved by 1% of the time
where the time goes in v1:
time: 55.7 us; the launch traced here: 55.5 us
  Pallas kernels  54.2 us (97%)
  local copies, waits for them, and re-layouts  1.32 us (2%)
    pallas_call x1, Pallas kernels, on_device(): pl.pallas_call(kernel, out_shape=jax.ShapeDtypeStruct((12, HALF), F32), i...  54.2 us
    unnamed x7, local copies, waits for them, and re-layouts  1.32 us

profile of v1, /device:TPU:8, one launch (start us, length us, event | category | flops | bytes accessed | tf_op | source)
XLA Modules:
  0.0 55.5 jit_solution(6300747579367380803)
XLA Ops:
  0.0 0.0 copy-start.2
  0.0 0.0 copy-start
  0.0 0.0 copy-start.1
  0.0 0.7 %copy-done.2 = s32[192]{0:T(256)S(1)} copy-done((s32[192]{0:T(256)S(1)}, s32[192]{0:T(256)}, u32[]{:S(2)}) %copy-start.2) | copy-done | bytes 792
  0.7 0.0 copy-done
  0.7 0.0 copy-done.1
  0.7 54.2 %estep.1 = f32[12,512]{1,0:T(8,128)S(1)} custom-call(bf16[96,4096]{1,0:T(8,128)(2,1)} %parts.1, bf16[12,4096]{1,0:T(8,128)(2,1)} %refs_in.1, s32[4,96]{1,0:T(4,128)S(1)} %bitcast.3, s32[2,9]{1,0:T(2,128)S(1)} %bitcast.4, s32[1,192]{1,0:T(1,128)S(1)} %bitcast.5), custom_call_target="tpu_custom_call" | custom-call | tf_op jit(solution)/shard_map/estep/pallas_call | solution.py:489
  54.9 0.6 %copy.7 = f32[12,512]{1,0:T(8,128)} copy(f32[12,512]{1,0:T(8,128)S(1)} %estep.1) | data formatting | bytes 49152
Async XLA Ops:
  0.0 0.7 %copy-start.2 = (s32[192]{0:T(256)S(1)}, s32[192]{0:T(256)}, u32[]{:S(2)}) copy-start(s32[192]{0:T(256)} %param.9) | copy-start | bytes 2308
  0.0 0.7 %copy-start = (s32[96,4]{0,1:T(4,128)S(1)}, s32[96,4]{0,1:T(4,128)}, u32[]{:S(2)}) copy-start(s32[96,4]{0,1:T(4,128)} %param.7) | copy-start | bytes 4612
  0.0 0.7 %copy-start.1 = (s32[9,2]{0,1:T(2,128)S(1)}, s32[9,2]{0,1:T(2,128)}, u32[]{:S(2)}) copy-start(s32[9,2]{0,1:T(2,128)} %param.8) | copy-start | bytes 220
